TPU v7x, 256 devices: a whole 4x4x8 slice. The times are simulated.
256 devices in a mesh: mp: 2 (over x_hi), tp: 16 (over z, core), dp: 8 (over y, x_lo).
Axes of the slice: x: 4 (x_hi: 2, x_lo: 2; x = x_hi * 2 + x_lo), y: 4, z: 8, core: 2. Of those that a mesh axis runs over, the one named last changes fastest.
Arguments:
- hidden: bfloat16 [2, 1024, 28672], P('mp', 'dp', 'tp'), may hold values from -8 to 8
- down_weight: bfloat16 [2, 28672, 8192], P('mp', 'tp', 'dp'), may hold values from -0.03125 to 0.03125
- whitening: bfloat16 [2, 8192, 8192], P('mp', 'dp', 'tp'), may hold values from -0.0625 to 0.0625
Outputs:
- cross: float32 [8192, 8192], P(('mp', 'dp'), 'tp')
All inputs are finite; a program needn't handle non-finite values.
Results may differ from a plain program's by a relative error of at most 0.0093.
Values may be sent and summed in bfloat16 or wider, within the bound.
A program may use at most 64 MiB of HBM per device.

v0:
```python
import math

import jax
import jax.numpy as jnp
from jax import lax
from jax.sharding import PartitionSpec as P


def from_partner(block, axis, distance):
    count = lax.axis_size(axis)
    route = []
    for low in range(count):
        high = low | 1 << distance
        if high != low and high < count:
            route += [(low, high), (high, low)]
    return lax.ppermute(block, axis, route)


def body(hidden, down_weight, whitening):
    acts = hidden[0]
    weights = down_weight[0]
    factor = whitening[0]
    partial_units = jnp.dot(
        lax.all_gather(acts, "dp", axis=0, tiled=True), weights, preferred_element_type=jnp.float32
    )
    outputs = lax.psum(partial_units, "tp").astype(jnp.bfloat16)
    total_tokens = outputs.shape[0]
    wide = outputs.astype(jnp.float32)
    mean = jnp.mean(wide, axis=0, keepdims=True)
    centered = (wide - mean).astype(jnp.bfloat16)
    rows = centered
    block = lax.psum_scatter(
        jnp.dot(rows, factor, preferred_element_type=jnp.float32),
        "dp",
        scatter_dimension=0,
        tiled=True,
    ).astype(jnp.bfloat16)
    scale = 1.0 / math.sqrt(total_tokens)
    own_model = lax.axis_index("mp")
    first = own_model == 0
    contract = (((0,), (0,)), ((), ()))
    half = block.shape[0] // 2
    give = lax.dynamic_slice_in_dim(block, (1 - own_model) * half, half, 0)
    received = from_partner(give, "mp", 0)
    keep = lax.dynamic_slice_in_dim(block, own_model * half, half, 0)
    llama_half = jnp.where(first, keep, received)
    qwen_half = jnp.where(first, received, keep)
    llama_all = lax.all_gather(llama_half, "tp", axis=1, tiled=True)
    rows = llama_all
    return (
        lax.psum_scatter(
            lax.dot_general(rows, qwen_half, contract, preferred_element_type=jnp.float32),
            ("mp", "dp"),
            scatter_dimension=0,
            tiled=True,
        )
        * scale
    )


def solution(mesh):
    placed = (P("mp", "dp", "tp"), P("mp", "tp", "dp"), P("mp", "dp", "tp"))
    return jax.shard_map(
        body, mesh=mesh, in_specs=placed, out_specs=P(("mp", "dp"), "tp"), check_vma=False
    )
```

profile of v0, /device:TPU:1, one launch (start us, length us, event | category | flops | bytes accessed | tf_op | source)
XLA Modules:
  0.0 641.3 jit_solution(8933854863904271175)
XLA Ops:
  6.5 0.0 copy-start
  6.5 0.0 all-gather.6.cloned.1.call-start
  6.5 0.7 all-gather.6.cloned.1.call-update
  7.3 0.0 reduce-scatter.3.cloned.1.call-start
  7.3 89.1 %all-gather.6.cloned.1.call-done = bf16[1,1024,1792]{2,1,0:T(8,128)(2,1)} async-done(((bf16[1,128,1792]{2,1,0:T(8,128)(2,1)}), bf16[1,1024,1792]{2,1,0:T(8,128)(2,1)}) %all-gather.6.cloned.1.call-update) | async-done | bytes 3670032 | tf_op jit(solution)/shard_map/all_gather | solution.py:24
  96.4 9.0 %fusion.1 = f32[1024,1024]{1,0:T(8,128)} fusion(bf16[1,1792,1024]{2,1,0:T(8,128)(2,1)} %param.4, bf16[1,1024,1792]{2,1,0:T(8,128)(2,1)} %all-gather.6.cloned.1.call-done), kind=kOutput, calls=%fused_computation.3 | convolution fusion | flops 3758096384 | bytes 11534336 | tf_op jit(solution)/shard_map/dot_general | solution.py:23
  105.4 63.2 %all-reduce.1 = bf16[1024,1024]{1,0:T(8,128)(2,1)S(1)} all-reduce(f32[1024,1024]{1,0:T(8,128)} %fusion.1), channel_id=1, replica_groups=mesh['mp'=2,'tp'=16,'dp'=8] {'tp'}, use_global_device_ids=true, to_apply=%region_0.0 | all-reduce | flops 1048576 | bytes 6291456 | tf_op jit(solution)/shard_map/psum | solution.py:26
  168.6 0.4 convert_reduce_fusion
  168.9 0.0 copy-done
  168.9 2.6 fusion.4
  171.5 0.0 reduce-scatter.3.cloned.1.call-update
  171.6 0.0 all-gather.4.cloned.1.call-start
  171.6 55.4 %reduce-scatter.3.cloned.1.call-done = f32[128,512]{1,0:T(8,128)} async-done(((f32[1024,512]{1,0:T(8,128)}), f32[128,512]{1,0:T(8,128)}) %reduce-scatter.3.cloned.1.call-update) | async-done | bytes 262160 | tf_op jit(solution)/shard_map/reduce_scatter | solution.py:32
  227.0 1.0 convert_element_type.15
  228.0 2.5 collective-permute-start
  230.5 2.2 collective-permute-done
  232.7 0.6 broadcast_select_fusion
  233.4 0.0 all-gather.4.cloned.1.call-update
  233.4 0.0 reduce-scatter.5.cloned.1.call-start
  233.4 39.8 %all-gather.4.cloned.1.call-done = bf16[64,8192]{1,0:T(8,128)(2,1)} async-done(((bf16[64,512]{1,0:T(8,128)(2,1)}), bf16[64,8192]{1,0:T(8,128)(2,1)}) %all-gather.4.cloned.1.call-update) | async-done | bytes 1048592 | tf_op jit(solution)/shard_map/all_gather | solution.py:48
  273.2 9.3 %fusion.9 = f32[8192,512]{1,0:T(8,128)} fusion(bf16[64,8192]{1,0:T(8,128)(2,1)} %all-gather.4.cloned.1.call-done, bf16[64,512]{1,0:T(8,128)(2,1)S(1)} %collective-permute-done, pred[]{:T(512)S(6)} %eq.3, bf16[128,512]{1,0:T(8,128)(2,1)S(1)} %convert_element_type.15, s32[]{:T(128)S(6)} %select_n.19), kind=kOutput, calls=%fused_computation.11 | convolution fusion | flops 536903680 | bytes 17956868 | tf_op jit(solution)/shard_map/dot_general | solution.py:52
  282.5 0.0 reduce-scatter.5.cloned.1.call-update
  282.5 349.9 %reduce-scatter.5.cloned.1.call-done = f32[512,512]{1,0:T(8,128)} async-done(((f32[8192,512]{1,0:T(8,128)}), f32[512,512]{1,0:T(8,128)}) %reduce-scatter.5.cloned.1.call-update) | async-done | bytes 1048592 | tf_op jit(solution)/shard_map/reduce_scatter | solution.py:51
  632.5 2.3 broadcast_multiply_fusion
  (2 shorter events, 0.0 us)
Async XLA Ops:
  6.5 162.4 %copy-start = (bf16[1,1024,512]{2,1,0:T(8,128)(2,1)S(1)}, bf16[1,1024,512]{2,1,0:T(8,128)(2,1)}, u32[]{:S(2)}) copy-start(bf16[1,1024,512]{2,1,0:T(8,128)(2,1)} %param.5) | copy-start | bytes 3145732
  6.5 89.8 %all-gather.6.cloned.1.call-start = ((), (), s32[]{:S(2)}) async-start(), calls=%async_computation.5 | async-start | bytes 4128768 | tf_op jit(solution)/shard_map/all_gather | solution.py:24
  7.3 219.7 %reduce-scatter.3.cloned.1.call-start = ((), (), s32[]{:S(2)}) async-start(), calls=%async_computation.2 | async-start | bytes 2359296 | tf_op jit(solution)/shard_map/reduce_scatter | solution.py:32
  171.6 101.6 %all-gather.4.cloned.1.call-start = ((), (), s32[]{:S(2)}) async-start(), calls=%async_computation.3 | async-start | bytes 1114112 | tf_op jit(solution)/shard_map/all_gather | solution.py:48
  228.0 4.7 collective-permute-start
  233.4 399.1 %reduce-scatter.5.cloned.1.call-start = ((), (), s32[]{:S(2)}) async-start(), calls=%async_computation.4 | async-start | bytes 17825792 | tf_op jit(solution)/shard_map/reduce_scatter | solution.py:51
Sparse Core Ops, SparseCore 0:
  9.1 87.1 all-gather.5
  171.7 55.2 reduce-scatter.2
  233.5 39.6 all-gather.3
  282.7 349.7 reduce-scatter.4
where the time goes:
time: 642 us; the launch traced here: 641 us
  waiting for transfers between devices  537 us (84%)
  blocking collectives  63.2 us (10%)
  matrix products  21 us (3%)
  between operations  13.2 us (2%)
    reduce_scatter x1, waiting for transfers between devices, body(): lax.psum_scatter(lax.dot_general(rows, qwen_half, contract, preferred_ele...  350 us
    all_gather x1, waiting for transfers between devices, body(): lax.all_gather(acts, 'dp', axis=0, tiled=True)  89.1 us
    psum x1, blocking collectives, body(): outputs = lax.psum(partial_units, 'tp').astype(jnp.bfloat16)  63.2 us
    reduce_scatter x1, waiting for transfers between devices, body(): lax.psum_scatter(jnp.dot(rows, factor, preferred_element_type=jnp.float32...  55.4 us
    all_gather x1, waiting for transfers between devices, body(): llama_all = lax.all_gather(llama_half, 'tp', axis=1, tiled=True)  39.8 us
  transfers between devices with their start and end apart: 5, of which 5 were waited for; matrix products, arithmetic and copies ran while one was open for 0% of the time, Pallas kernels for 0%

commit v1 on v0

v1 whole, which is shorter than its diff:
```python
import math

import jax
import jax.numpy as jnp
from jax import lax
from jax.experimental import pallas as pl
from jax.experimental.pallas import tpu as pltpu
from jax.sharding import PartitionSpec as P

MESH = pl.DeviceIdType.MESH
F32, BF16 = jnp.float32, jnp.bfloat16
TILE = 256
SHIFTS = (0, -1, 1, 2)
PENDING = ((), (12,), (13,), (3, 8, 4, 9))
ORDER = (
    "near", 0, 0, "far", 1, 1, 0, 2, 0, 2, 0, 1, 0, 0, 1, 2, 1, 0, 3, 3, 1, 2, 1, 2, 1, 3, 2, 2, 3, 2, 3, 3, 3, 3,
)


def kernel(
    hid, wgt, fac, out,
    acts, weights, factor, sums, own, give, take, parts, reduced, outs,
    wpart, wown, wland, white, qwen, llama,
    load_sem, near_sem, sum_sem, pair_sem, ring_sem, all_sem, core_sem, dp_sem, mp_sem, row_sem, spread_sem, last_sem,
):
    mp, tp, dp = lax.axis_index("mp"), lax.axis_index("tp"), lax.axis_index("dp")
    z, core = tp // 2, tp % 2
    y, xlo = dp // 2, dp % 2
    tokens = hid.shape[1]
    half = tokens // 2
    group_rows = 2 * tokens
    piece = group_rows // 8
    width = wgt.shape[2]
    side = width // 2
    cols = fac.shape[2]

    def at(**coords):
        return {"mp": coords.get("mp", mp), "tp": coords.get("tp", tp), "dp": coords.get("dp", dp)}

    def rem(value, count):
        return lax.rem(value + count, count)

    started = []

    def copy(src, dst, sem, index, target, there=None):
        return pltpu.make_async_remote_copy(
            src_ref=src, dst_ref=dst, send_sem=sem.at[(0, *index)], recv_sem=sem.at[(1, *(there or index))],
            device_id=target, device_id_type=MESH,
        )

    def send(*args, **kw):
        c = copy(*args, **kw)
        c.start()
        started.append(c)

    def arrived(dst, sem, index):
        copy(dst, dst, sem, index, at()).wait_recv()

    row0 = pl.multiple_of(dp * tokens, tokens)
    loads = [
        pltpu.make_async_copy(hid.at[0], acts.at[pl.ds(row0, tokens)], load_sem.at[0]),
        pltpu.make_async_copy(wgt.at[0], weights, load_sem.at[1]),
        pltpu.make_async_copy(fac.at[0], factor, load_sem.at[2]),
    ]
    for load in loads:
        load.start()

    barrier = pltpu.get_barrier_semaphore()
    row_source = mp * 8 + dp
    greet = [at(dp=rem(dp + o, 8)) for o in range(1, 8)]
    greet += [at(tp=rem(tp + 2 * o, 16)) for o in range(1, 8)]
    greet += [at(tp=tp + 1 - 2 * core)]
    greet += [at(mp=1 - mp, dp=rem(dp + o, 8)) for o in range(8)]
    for target in greet:
        pl.semaphore_signal(barrier, inc=1, device_id=target, device_id_type=MESH)
    alone = (mp == 0) & (dp == 0) & (tp == 0)

    @pl.when(jnp.logical_not(alone))
    def _():
        pl.semaphore_signal(
            barrier, inc=1, device_id=at(mp=0, dp=z, tp=row_source), device_id_type=MESH
        )

    loads[0].wait()
    sums[dp] = jnp.sum(acts[pl.ds(row0, tokens), :].astype(F32), axis=0, keepdims=True)

    extra = jnp.where(mp == 0, jnp.where(alone, 1, 2), 0)
    pl.semaphore_wait(barrier, len(greet) + extra)

    for o in range(1, 8):
        send(sums.at[dp], sums.at[dp], sum_sem, (o,), at(dp=rem(dp + o, 8)))

    up, down, across = at(dp=rem(dp + 2, 8)), at(dp=rem(dp - 2, 8)), at(dp=dp + 1 - 2 * xlo)

    def rows(dy, other, which):
        x = 1 - xlo if other else xlo
        start = (rem(y + dy + 4, 4) * 2 + x) * tokens + which * half
        return acts.at[pl.ds(pl.multiple_of(start, half), half)]

    hops = {
        0: (up, 0, 0, 0), 1: (up, 0, 0, 1), 2: (up, 0, 1, 0), 3: (up, -1, 0, 0), 4: (up, -1, 1, 0),
        5: (down, 0, 0, 1), 6: (down, 0, 0, 0), 7: (down, 0, 1, 1), 8: (down, 1, 0, 1), 9: (down, 1, 1, 1),
        10: (across, 0, 0, 0), 11: (across, 0, 0, 1), 12: (across, -1, 0, 1), 13: (across, 1, 0, 0),
    }

    def hop(index):
        target, dy, other, which = hops[index]
        block = rows(dy, other, which)
        send(block, block, near_sem, (index,), target)

    def landed(index):
        target, dy, other, which = hops[index]
        if target is up:
            block = rows(dy - 1, other, which)
        elif target is down:
            block = rows(dy + 1, other, which)
        else:
            block = rows(dy, 1 - other, which)
        arrived(block, near_sem, (index,))

    for index in (10, 0, 5, 11, 1, 6):
        hop(index)

    loads[1].wait()
    for o in range(1, 8):
        arrived(sums.at[rem(dp - o, 8)], sum_sem, (o,))
    mean = jnp.sum(sums[...], axis=0) * (1.0 / 1024)
    high = mean.astype(BF16).astype(F32)
    line = lax.broadcasted_iota(jnp.int32, (16, mean.shape[1]), 0)
    pair = jnp.where(line == 0, high, jnp.where(line == 1, mean - high, 0.0)).astype(BF16)
    shift = jnp.sum(jnp.dot(pair, weights[...], preferred_element_type=F32), axis=0, keepdims=True)
    own_shift = jnp.where(core == 0, shift[:, :side], shift[:, side:])
    other_shift = jnp.where(core == 0, shift[:, side:], shift[:, :side])

    sibling = at(tp=tp + 1 - 2 * core)
    sign = 1 - 2 * core
    ahead, behind = at(tp=rem(tp + 2 * sign, 16)), at(tp=rem(tp - 2 * sign, 16))

    def group(g):
        base = rem(y + SHIFTS[g], 4) * group_rows
        base = pl.multiple_of(base, group_rows)
        block = acts.at[pl.ds(base, group_rows)]

        def partial(dst, first, offset):
            for n in range(side // TILE):
                columns = pl.ds(pl.multiple_of(first + n * TILE, TILE), TILE)
                here = pl.ds(n * TILE, TILE)
                dst[g, :, here] = (
                    jnp.dot(block[...], weights[:, columns], preferred_element_type=F32)
                    - offset[:, n * TILE:(n + 1) * TILE]
                )

        for index in PENDING[g]:
            landed(index)
        partial(give, (1 - core) * side, other_shift)
        send(give.at[g], take.at[g], pair_sem, (g,), sibling)
        partial(own, core * side, own_shift)
        yield
        arrived(take.at[g], pair_sem, (g,))
        total = own[g] + take[g]
        own[g] = total
        parts[g] = total.astype(BF16)
        for o in (4, 3, 5, 2, 6, 1, 7):
            to = rem(z + o, 8)
            send(
                parts.at[g, pl.ds(pl.multiple_of(to * piece, piece), piece)], reduced.at[g, o],
                ring_sem, (g, o), at(tp=rem(tp + 2 * o, 16)),
            )
        yield
        here = pl.ds(pl.multiple_of(z * piece, piece), piece)
        result = own[g, here, :]
        for o in (1, 7, 2, 6, 3, 5, 4):
            arrived(reduced.at[g, o], ring_sem, (g, o))
            result = result + reduced[g, o].astype(F32)
        mine = pl.ds(pl.multiple_of(core * side, side), side)

        def chunk(distance):
            start = base + rem(z + distance + 8, 8) * piece
            return outs.at[pl.ds(pl.multiple_of(start, piece), piece), mine]

        outs[pl.ds(pl.multiple_of(base + z * piece, piece), piece), mine] = result.astype(BF16)
        send(chunk(0), chunk(0), all_sem, (g, 1), ahead)
        send(chunk(0), chunk(0), all_sem, (g, 5), behind)
        for step in (1, 2, 3):
            yield
            block_a = chunk(-sign * step)
            arrived(block_a, all_sem, (g, step))
            send(block_a, block_a, all_sem, (g, step + 1), ahead)
            block_b = chunk(sign * step)
            arrived(block_b, all_sem, (g, 4 + step))
            if step < 3:
                send(block_b, block_b, all_sem, (g, 5 + step), behind)
        yield
        arrived(chunk(-sign * 4), all_sem, (g, 4))
        whole = outs.at[pl.ds(base, group_rows), mine]
        send(whole, whole, core_sem, (g,), sibling)
        yield
        theirs = pl.ds(pl.multiple_of((1 - core) * side, side), side)
        arrived(outs.at[pl.ds(base, group_rows), theirs], core_sem, (g,))
        if g == 0:
            loads[2].wait()
        for n in range(cols // TILE):
            here = pl.ds(n * TILE, TILE)
            product = jnp.dot(
                outs[pl.ds(base, group_rows), :], factor[:, here], preferred_element_type=F32
            )
            if g == 0:
                mine_first = xlo == 0
                wown[:, here] = jnp.where(mine_first, product[:tokens], product[tokens:])
            wpart[g, :, here] = product.astype(BF16)
        owner = rem(y + SHIFTS[g] + 4, 4) * 2
        for cross in (0, 1):
            if g == 0 and cross == 0:
                continue
            x = 1 - xlo if cross else xlo
            send(
                wpart.at[g, pl.ds(pl.multiple_of(x * tokens, tokens), tokens)], wland.at[g, cross],
                dp_sem, (g, cross), at(dp=owner + x),
            )
        yield

    groups = [group(g) for g in range(4)]
    for name in ORDER:
        if name == "near":
            for incoming, outgoing in ((10, 2), (0, 3), (5, 8), (11, 7), (1, 12), (6, 13)):
                landed(incoming)
                hop(outgoing)
        elif name == "far":
            for incoming, outgoing in ((2, 4), (7, 9)):
                landed(incoming)
                hop(outgoing)
        else:
            next(groups[name])

    result = wown[...]
    for g in range(4):
        for cross in (0, 1):
            if g or cross:
                arrived(wland.at[g, cross], dp_sem, (g, cross))
                result = result + wland[g, cross].astype(F32)
    white[...] = result.astype(BF16)

    place = pl.ds(row0, tokens)

    def qwen_sends():
        return [
            copy(white, qwen.at[place], mp_sem, (a, o), at(mp=a, dp=rem(dp + o, 8)), (0, o))
            for o in (4, 5, 3, 6, 2, 7, 1, 0) for a in (0, 1) if a == 0 or o
        ]

    def llama_send(c):
        return copy(
            white.at[pl.ds(c * half, half)], llama.at[dp, c], row_sem, (c,),
            at(mp=tp // 8, dp=rem(tp, 8), tp=2 * dp + c), (0,),
        )

    @pl.when(mp == 1)
    def _():
        for c in qwen_sends():
            c.start()
        local = pltpu.make_async_copy(white, qwen.at[place], load_sem.at[3])
        local.start()
        local.wait()

    @pl.when(mp == 0)
    def _():
        llama_send(1).start()

        @pl.when(alone)
        def _():
            local = pltpu.make_async_copy(white.at[pl.ds(0, half)], llama.at[0, 0], load_sem.at[3])
            local.start()
            local.wait()

        @pl.when(jnp.logical_not(alone))
        def _():
            llama_send(0).start()

    @pl.when(jnp.logical_not(alone))
    def _():
        arrived(llama.at[z, core], row_sem, (0,))

    def spread(distance):
        return llama.at[rem(z + distance + 8, 8), core]

    send(spread(0), spread(0), spread_sem, (1,), ahead)
    send(spread(0), spread(0), spread_sem, (5,), behind)
    for step in (1, 2, 3):
        block_a = spread(-sign * step)
        arrived(block_a, spread_sem, (step,))
        send(block_a, block_a, spread_sem, (step + 1,), ahead)
        block_b = spread(sign * step)
        arrived(block_b, spread_sem, (4 + step,))
        if step < 3:
            send(block_b, block_b, spread_sem, (5 + step,), behind)
    arrived(spread(-sign * 4), spread_sem, (4,))
    send(llama.at[:, core], llama.at[:, core], last_sem, (0,), sibling)
    for o in range(1, 8):
        source = pl.multiple_of(rem(dp - o, 8) * tokens, tokens)
        arrived(qwen.at[pl.ds(source, tokens)], mp_sem, (0, o))

    @pl.when(mp == 0)
    def _():
        arrived(qwen.at[place], mp_sem, (0, 0))

    arrived(llama.at[:, 1 - core], last_sem, (0,))
    left = llama[...].reshape(8 * tokens, cols)
    for n in range(cols // TILE):
        here = pl.ds(n * TILE, TILE)
        out[:, here] = lax.dot_general(
            left, qwen[:, here], (((0,), (0,)), ((), ())), preferred_element_type=F32
        ) * (1.0 / math.sqrt(8 * tokens))

    for c in started:
        c.wait_send()

    @pl.when(mp == 1)
    def _():
        for c in qwen_sends():
            c.wait_send()

    @pl.when(mp == 0)
    def _():
        llama_send(1).wait_send()

        @pl.when(jnp.logical_not(alone))
        def _():
            llama_send(0).wait_send()


def body(hidden, down_weight, whitening):
    tokens, units = hidden.shape[1:]
    width, cols = down_weight.shape[2], whitening.shape[2]
    group_rows, side = 2 * tokens, width // 2
    piece = group_rows // 8
    dma = pltpu.SemaphoreType.DMA
    anywhere = pl.BlockSpec(memory_space=pl.ANY)
    return pl.pallas_call(
        kernel,
        out_shape=jax.ShapeDtypeStruct((cols, cols), F32),
        in_specs=[anywhere] * 3,
        out_specs=pl.BlockSpec(memory_space=pltpu.VMEM),
        scratch_shapes=[
            pltpu.VMEM((8 * tokens, units), BF16),
            pltpu.VMEM((units, width), BF16),
            pltpu.VMEM((width, cols), BF16),
            pltpu.VMEM((8, 1, units), F32),
            pltpu.VMEM((4, group_rows, side), F32),
            pltpu.VMEM((4, group_rows, side), F32),
            pltpu.VMEM((4, group_rows, side), F32),
            pltpu.VMEM((4, group_rows, side), BF16),
            pltpu.VMEM((4, 8, piece, side), BF16),
            pltpu.VMEM((8 * tokens, width), BF16),
            pltpu.VMEM((4, group_rows, cols), BF16),
            pltpu.VMEM((tokens, cols), F32),
            pltpu.VMEM((4, 2, tokens, cols), BF16),
            pltpu.VMEM((tokens, cols), BF16),
            pltpu.VMEM((8 * tokens, cols), BF16),
            pltpu.VMEM((8, 2, tokens // 2, cols), BF16),
            dma((4,)),
            dma((2, 14)),
            dma((2, 8)),
            dma((2, 4)),
            dma((2, 4, 8)),
            dma((2, 4, 8)),
            dma((2, 4)),
            dma((2, 4, 2)),
            dma((2, 2, 8)),
            dma((2, 2)),
            dma((2, 8)),
            dma((2, 1)),
        ],
        compiler_params=pltpu.CompilerParams(
            collective_id=0, has_side_effects=True, vmem_limit_bytes=58 * 2**20
        ),
        cost_estimate=pl.CostEstimate(
            flops=5_400_000_000, bytes_accessed=6_000_000, transcendentals=0
        ),
    )(hidden, down_weight, whitening)


def solution(mesh):
    placed = (P("mp", "dp", "tp"), P("mp", "tp", "dp"), P("mp", "dp", "tp"))
    return jax.shard_map(
        body, mesh=mesh, in_specs=placed, out_specs=P(("mp", "dp"), "tp"), check_vma=False
    )
```

time: 642 us -> 130 us (0.20)
  waiting for transfers between devices: 537 us -> 0 us
  Pallas kernels: 0 us -> 127 us
  blocking collectives: 63.2 us -> 0 us
  matrix products: 21 us -> 0 us
  between operations: 13.2 us -> 0.01 us
    reduce_scatter x2 -> x0, waiting for transfers between devices: 405 us -> none  [the longest x1 350 us: body(): lax.psum_scatter(lax.dot_general(rows, qwen_half, contract, preferred_ele...]
    all_gather x2 -> x0, waiting for transfers between devices: 129 us -> none  [the longest x1 89.1 us: body(): lax.all_gather(acts, 'dp', axis=0, tiled=True)]
    pallas_call x0 -> x1, Pallas kernels: none -> 127 us  [body(): pl.pallas_call(kernel, out_shape=jax.ShapeDtypeStruct((cols, cols), F32),...]
    psum x1 -> x0, blocking collectives: 63.2 us -> none  [body(): outputs = lax.psum(partial_units, 'tp').astype(jnp.bfloat16)]
    dot_general x3 -> x0, matrix products: 21 us -> none  [the longest x1 9.32 us: body(): lax.dot_general(rows, qwen_half, contract, preferred_element_type=jnp.flo...]
  transfers between devices with their start and end apart: 5 -> 0, of which waited for: 5 -> 0; matrix products, arithmetic and copies ran while one was open for 0% -> 0% of each run, Pallas kernels for 0% -> 0%
where the time goes in v1:
time: 130 us; the launch traced here: 129 us
  Pallas kernels  127 us (98%)
  local copies, waits for them, and re-layouts  2.26 us (2%)
    pallas_call x1, Pallas kernels, body(): pl.pallas_call(kernel, out_shape=jax.ShapeDtypeStruct((cols, cols), F32),...  127 us

profile of v1, /device:TPU:1, one launch (start us, length us, event | category | flops | bytes accessed | tf_op | source)
XLA Modules:
  0.0 129.4 jit_solution(4255554709073773119)
XLA Ops:
  0.0 127.2 %shard_map.37 = f32[512,512]{1,0:T(8,128)} custom-call(bf16[1,128,1792]{2,1,0:T(8,128)(2,1)} %hid.1, bf16[1,1792,1024]{2,1,0:T(8,128)(2,1)} %wgt.1, bf16[1,1024,512]{2,1,0:T(8,128)(2,1)} %fac.1), custom_call_target="tpu_custom_call" | custom-call | flops 5400000000 | bytes 6000000 | tf_op jit(solution)/shard_map/pallas_call | solution.py:338
  127.2 2.3 %copy.5 = f32[512,512]{1,0:T(8,128)} copy(f32[512,512]{1,0:T(8,128)} %shard_map.37) | data formatting | bytes 2097152

commit v2 on v1

v2 whole, which is shorter than its diff:
```python
import math

import jax
import jax.numpy as jnp
from jax import lax
from jax.experimental import pallas as pl
from jax.experimental.pallas import tpu as pltpu
from jax.sharding import PartitionSpec as P

MESH = pl.DeviceIdType.MESH
F32, BF16 = jnp.float32, jnp.bfloat16
TILE = 256
GROUPS = ((0, 0), (0, 1), (-1, 0), (-1, 1), (1, 0), (1, 1), (2, 0), (2, 1))
DELTAS = (0, -1, 1, 2)
FORWARD = {
    "near": ((10, 2), (0, 3), (5, 8)), "next": ((11, 7), (1, 12), (6, 13)), "far": ((2, 4),), "last": ((7, 9),),
}
PENDING = ((), (), (), (12,), (), (13,), (3, 8), (4, 9))
ORDER = (
    0, 0, "near", 0, "next", 1, 2, 4, 1, 2, 0, "far", 4, 3, 1, 2, 3, "last", 4, 0, 6, 2, 1, 5, 4, 3, 0, 6, 5, 7, 1,
    4, 0, 7, 6, 3, 5, 1, 2, 4, 1, 7, 6, 4, 3, 5, 2, 7, 2, 6, 3, 5, 3, 7, 6, 5, 6, 7, 5, 7,
)


def kernel(
    hid, wgt, fac, out,
    acts, weights, factor, sums, own, give, take, parts, reduced, outs,
    wpart, land, white, rowpart, qwen, llama,
    load_sem, near_sem, sum_sem, pair_sem, ring_sem, all_sem, core_sem, dp_sem, mp_sem, row_sem, spread_sem, last_sem,
):
    mp, tp, dp = lax.axis_index("mp"), lax.axis_index("tp"), lax.axis_index("dp")
    z, core = tp // 2, tp % 2
    y, xlo = dp // 2, dp % 2
    tokens = hid.shape[1]
    half = tokens // 2
    width = wgt.shape[2]
    side = width // 2
    cols = fac.shape[2]

    def at(**coords):
        return {"mp": coords.get("mp", mp), "tp": coords.get("tp", tp), "dp": coords.get("dp", dp)}

    def rem(value, count):
        return lax.rem(value + count, count)

    started = []

    def copy(src, dst, sem, index, target, there=None):
        return pltpu.make_async_remote_copy(
            src_ref=src, dst_ref=dst, send_sem=sem.at[(0, *index)], recv_sem=sem.at[(1, *(there or index))],
            device_id=target, device_id_type=MESH,
        )

    def send(*args, **kw):
        c = copy(*args, **kw)
        c.start()
        started.append(c)

    def arrived(dst, sem, index):
        copy(dst, dst, sem, index, at()).wait_recv()

    row0 = pl.multiple_of(dp * tokens, tokens)
    loads = [
        pltpu.make_async_copy(hid.at[0], acts.at[pl.ds(row0, tokens)], load_sem.at[0]),
        pltpu.make_async_copy(wgt.at[0], weights, load_sem.at[1]),
        pltpu.make_async_copy(fac.at[0], factor, load_sem.at[2]),
    ]
    for load in loads:
        load.start()

    barrier = pltpu.get_barrier_semaphore()
    row_source = mp * 8 + dp
    greet = [at(dp=rem(dp + o, 8)) for o in range(1, 8)]
    greet += [at(tp=rem(tp + 2 * o, 16)) for o in (1, 2, -1, -2)]
    greet += [at(tp=tp + 1 - 2 * core)]
    greet += [at(mp=1 - mp, dp=rem(dp + o, 8)) for o in range(8)]
    for target in greet:
        pl.semaphore_signal(barrier, inc=1, device_id=target, device_id_type=MESH)
    alone = (mp == 0) & (dp == 0) & (tp == 0)

    @pl.when(jnp.logical_not(alone))
    def _():
        pl.semaphore_signal(
            barrier, inc=1, device_id=at(mp=0, dp=z, tp=row_source), device_id_type=MESH
        )

    loads[0].wait()
    sums[dp] = jnp.sum(acts[pl.ds(row0, tokens), :].astype(F32), axis=0, keepdims=True)

    extra = jnp.where(mp == 0, jnp.where(alone, 1, 2), 0)
    pl.semaphore_wait(barrier, len(greet) + extra)

    for o in range(1, 8):
        send(sums.at[dp], sums.at[dp], sum_sem, (o,), at(dp=rem(dp + o, 8)))

    up, down, across = at(dp=rem(dp + 2, 8)), at(dp=rem(dp - 2, 8)), at(dp=dp + 1 - 2 * xlo)

    def rows(dy, other, which):
        x = 1 - xlo if other else xlo
        start = (rem(y + dy + 4, 4) * 2 + x) * tokens + which * half
        return acts.at[pl.ds(pl.multiple_of(start, half), half)]

    hops = {
        0: (up, 0, 0, 0), 1: (up, 0, 0, 1), 2: (up, 0, 1, 0), 3: (up, -1, 0, 0), 4: (up, -1, 1, 0),
        5: (down, 0, 0, 1), 6: (down, 0, 0, 0), 7: (down, 0, 1, 1), 8: (down, 1, 0, 1), 9: (down, 1, 1, 1),
        10: (across, 0, 0, 0), 11: (across, 0, 0, 1), 12: (across, -1, 0, 1), 13: (across, 1, 0, 0),
    }

    def hop(index):
        target, dy, other, which = hops[index]
        block = rows(dy, other, which)
        send(block, block, near_sem, (index,), target)

    def landed(index):
        target, dy, other, which = hops[index]
        if target is up:
            block = rows(dy - 1, other, which)
        elif target is down:
            block = rows(dy + 1, other, which)
        else:
            block = rows(dy, 1 - other, which)
        arrived(block, near_sem, (index,))

    for index in (10, 0, 5, 11, 1, 6):
        hop(index)

    loads[1].wait()
    for o in range(1, 8):
        arrived(sums.at[rem(dp - o, 8)], sum_sem, (o,))
    mean = jnp.sum(sums[...], axis=0) * (1.0 / 1024)
    high = mean.astype(BF16).astype(F32)
    line = lax.broadcasted_iota(jnp.int32, (16, mean.shape[1]), 0)
    pair = jnp.where(line == 0, high, jnp.where(line == 1, mean - high, 0.0)).astype(BF16)
    shift = jnp.sum(jnp.dot(pair, weights[...], preferred_element_type=F32), axis=0, keepdims=True)
    own_shift = jnp.where(core == 0, shift[:, :side], shift[:, side:])
    other_shift = jnp.where(core == 0, shift[:, side:], shift[:, :side])

    sibling = at(tp=tp + 1 - 2 * core)
    sign = 1 - 2 * core

    def along(distance):
        return at(tp=rem(tp + 2 * sign * distance + 16, 16))

    def gather(chunk, sem, index):
        for slot, distance in ((2, 2), (3, -2), (0, 1), (1, -1)):
            send(chunk(0), chunk(0), sem, (*index, slot), along(distance))
        yield
        arrived(chunk(-2), sem, (*index, 2))
        send(chunk(-2), chunk(-2), sem, (*index, 5), along(2))
        send(chunk(-2), chunk(-2), sem, (*index, 4), along(1))
        arrived(chunk(2), sem, (*index, 3))
        send(chunk(2), chunk(2), sem, (*index, 6), along(-1))
        arrived(chunk(-1), sem, (*index, 0))
        arrived(chunk(1), sem, (*index, 1))
        yield
        for slot, distance in ((4, -3), (6, 3), (5, -4)):
            arrived(chunk(distance), sem, (*index, slot))

    def group(g):
        delta, part = GROUPS[g]
        count = tokens if part is not None else 2 * tokens
        piece = count // 8
        base = rem(y + delta + 4, 4) * 2 * tokens
        if part is not None:
            base = base + (1 - xlo if part else xlo) * tokens
        base = pl.multiple_of(base, tokens)
        block = acts.at[pl.ds(base, count)]
        span = pl.ds(0, count)
        for index in PENDING[g]:
            landed(index)

        def partial(dst, first, offset):
            for n in range(side // TILE):
                columns = pl.ds(pl.multiple_of(first + n * TILE, TILE), TILE)
                dst[g, span, pl.ds(n * TILE, TILE)] = (
                    jnp.dot(block[...], weights[:, columns], preferred_element_type=F32)
                    - offset[:, n * TILE:(n + 1) * TILE]
                )

        partial(give, (1 - core) * side, other_shift)
        send(give.at[g, span], take.at[g, span], pair_sem, (g,), sibling)
        partial(own, core * side, own_shift)
        yield
        arrived(take.at[g, span], pair_sem, (g,))
        total = own[g, span, :] + take[g, span, :]
        own[g, span, :] = total
        parts[g, span, :] = total.astype(BF16)

        def rows_for(distance):
            start = rem(z + sign * distance + 8, 8) * piece
            return pl.ds(pl.multiple_of(start, piece), piece)

        def slot_of(slot):
            return reduced.at[g, slot, pl.ds(0, piece)]

        def to_slot(slot, owner, target):
            send(parts.at[g, rows_for(owner)], slot_of(slot), ring_sem, (g, slot), along(target))

        def add(start, slots):
            value = start
            for slot in slots:
                arrived(slot_of(slot), ring_sem, (g, slot))
                value = value + reduced[g, slot, pl.ds(0, piece), :].astype(F32)
            return value

        for slot, owner, target in ((1, 4, 2), (0, 3, 1), (2, -3, -1), (3, 1, 1), (4, -1, -1)):
            to_slot(slot, owner, target)
        yield
        parts[g, rows_for(-2), :] = add(own[g, rows_for(-2), :], (2,)).astype(BF16)
        to_slot(6, -2, -2)
        parts[g, rows_for(2), :] = add(own[g, rows_for(2), :], (0, 1)).astype(BF16)
        to_slot(5, 2, 2)
        yield
        result = add(own[g, rows_for(0), :], (3, 4, 6, 5))
        mine = pl.ds(pl.multiple_of(core * side, side), side)

        def chunk(distance):
            start = base + rem(z + sign * distance + 8, 8) * piece
            return outs.at[pl.ds(pl.multiple_of(start, piece), piece), mine]

        outs[pl.ds(pl.multiple_of(base + z * piece, piece), piece), mine] = result.astype(BF16)
        yield from gather(chunk, all_sem, (g,))
        whole = outs.at[pl.ds(base, count), mine]
        send(whole, whole, core_sem, (g,), sibling)
        yield
        theirs = pl.ds(pl.multiple_of((1 - core) * side, side), side)
        arrived(outs.at[pl.ds(base, count), theirs], core_sem, (g,))
        if g == 0:
            loads[2].wait()
        for n in range(cols // TILE):
            here = pl.ds(n * TILE, TILE)
            wpart[g, span, here] = jnp.dot(
                outs[pl.ds(base, count), :], factor[:, here], preferred_element_type=F32
            ).astype(BF16)
        owner = rem(y + delta + 4, 4) * 2
        d = DELTAS.index(delta)
        for cross in ((0, 1) if part is None else (part,)):
            x = 1 - xlo if cross else xlo
            first = x * tokens if part is None else 0

            def half_to(h, d=d, cross=cross, x=x, first=first):
                slot = jnp.where(mp == 0, h, 2)
                return copy(
                    wpart.at[g, pl.ds(pl.multiple_of(first + h * half, half), half)], land.at[slot, d, cross],
                    dp_sem, (h, d, cross), at(mp=mp * h, dp=owner + x), (slot, d, cross),
                )

            if d or cross:
                for h in (0, 1):
                    c = half_to(h)
                    c.start()
                    started.append(c)
            else:
                first = pl.multiple_of(first, tokens)

                @pl.when(mp == 0)
                def _():
                    for h in (0, 1):
                        land[h, 0, 0] = wpart[g, pl.ds(first + h * half, half), :]

                @pl.when(mp == 1)
                def _():
                    half_to(0).start()
                    land[2, 0, 0] = wpart[g, pl.ds(first + half, half), :]

                late.append(half_to(0))
        yield

    late = []
    groups = [group(g) for g in range(len(GROUPS))]
    for name in ORDER:
        if name in FORWARD:
            for incoming, outgoing in FORWARD[name]:
                landed(incoming)
                hop(outgoing)
        else:
            next(groups[name])

    slots = [(d, cross) for d in range(4) for cross in (0, 1)]

    def llama_send(c):
        return copy(
            rowpart.at[c], llama.at[dp, c], row_sem, (c,), at(mp=tp // 8, dp=rem(tp, 8), tp=2 * dp + c), (0,)
        )

    @pl.when(mp == 0)
    def _():
        for h in (0, 1):
            for d, cross in slots[1:]:
                arrived(land.at[h, d, cross], dp_sem, (h, d, cross))
            value = land[h, 0, 0].astype(F32)
            for d, cross in slots[1:]:
                value = value + land[h, d, cross].astype(F32)
            rowpart[h] = value.astype(BF16)
            if h == 1:
                llama_send(1).start()
            else:

                @pl.when(alone)
                def _():
                    local = pltpu.make_async_copy(rowpart.at[0], llama.at[0, 0], load_sem.at[3])
                    local.start()
                    local.wait()

                @pl.when(jnp.logical_not(alone))
                def _():
                    llama_send(0).start()

        arrived(land.at[2, 0, 0], dp_sem, (2, 0, 0))

    for d, cross in slots[1:]:
        arrived(land.at[2, d, cross], dp_sem, (2, d, cross))
    value = land[2, 0, 0].astype(F32)
    for d, cross in slots[1:]:
        value = value + land[2, d, cross].astype(F32)
    white[...] = value.astype(BF16)

    @pl.when(jnp.logical_not(alone))
    def _():
        arrived(llama.at[z, core], row_sem, (0,))

    def spread(distance):
        return llama.at[rem(z + sign * distance + 8, 8), core]

    def to_sibling(distances):
        for n in distances:
            send(spread(n), spread(n), last_sem, (n + 4,), sibling)

    spreading = gather(spread, spread_sem, ())
    next(spreading)
    for o in (4, 5, 3, 6, 2, 7, 1, 0):
        for other in (1, 0):
            if o or other:
                send(
                    white, qwen.at[dp, mp], mp_sem, (other, o),
                    at(mp=1 - mp if other else mp, dp=rem(dp + o, 8)),
                )
    qwen[dp, mp] = white[...]

    to_sibling((0,))
    next(spreading)
    to_sibling((-2, 2, -1, 1))
    for _ in spreading:
        pass
    to_sibling((-3, 3, -4))
    for other in (0, 1):
        for o in range(8):
            if o or other:
                source = qwen.at[rem(dp - o + 8, 8), 1 - mp if other else mp]
                arrived(source, mp_sem, (other, o))
    for n in (0, -2, 2, -1, 1, -3, 3, -4):
        theirs = llama.at[rem(z - sign * n + 8, 8), 1 - core]
        arrived(theirs, last_sem, (n + 4,))
    left = llama[...].reshape(8 * tokens, cols)
    for n in range(cols // TILE):
        here = pl.ds(n * TILE, TILE)
        out[:, here] = lax.dot_general(
            left, qwen[:, :, :, here].reshape(8 * tokens, TILE), (((0,), (0,)), ((), ())),
            preferred_element_type=F32,
        ) * (1.0 / math.sqrt(8 * tokens))

    for c in started:
        c.wait_send()

    @pl.when(mp == 1)
    def _():
        for c in late:
            c.wait_send()

    @pl.when(mp == 0)
    def _():
        llama_send(1).wait_send()

        @pl.when(jnp.logical_not(alone))
        def _():
            llama_send(0).wait_send()


def body(hidden, down_weight, whitening):
    tokens, units = hidden.shape[1:]
    width, cols = down_weight.shape[2], whitening.shape[2]
    group_rows, side = 2 * tokens, width // 2
    piece, count = group_rows // 8, len(GROUPS)
    dma = pltpu.SemaphoreType.DMA
    anywhere = pl.BlockSpec(memory_space=pl.ANY)
    return pl.pallas_call(
        kernel,
        out_shape=jax.ShapeDtypeStruct((cols, cols), F32),
        in_specs=[anywhere] * 3,
        out_specs=pl.BlockSpec(memory_space=pltpu.VMEM),
        scratch_shapes=[
            pltpu.VMEM((8 * tokens, units), BF16),
            pltpu.VMEM((units, width), BF16),
            pltpu.VMEM((width, cols), BF16),
            pltpu.VMEM((8, 1, units), F32),
            pltpu.VMEM((count, group_rows, side), F32),
            pltpu.VMEM((count, group_rows, side), F32),
            pltpu.VMEM((count, group_rows, side), F32),
            pltpu.VMEM((count, group_rows, side), BF16),
            pltpu.VMEM((count, 7, piece, side), BF16),
            pltpu.VMEM((8 * tokens, width), BF16),
            pltpu.VMEM((count, group_rows, cols), BF16),
            pltpu.VMEM((3, 4, 2, tokens // 2, cols), BF16),
            pltpu.VMEM((tokens // 2, cols), BF16),
            pltpu.VMEM((2, tokens // 2, cols), BF16),
            pltpu.VMEM((8, 2, tokens // 2, cols), BF16),
            pltpu.VMEM((8, 2, tokens // 2, cols), BF16),
            dma((4,)),
            dma((2, 14)),
            dma((2, 8)),
            dma((2, count)),
            dma((2, count, 7)),
            dma((2, count, 7)),
            dma((2, count)),
            dma((2, 3, 4, 2)),
            dma((2, 2, 8)),
            dma((2, 2)),
            dma((2, 7)),
            dma((2, 8)),
        ],
        compiler_params=pltpu.CompilerParams(
            collective_id=0, has_side_effects=True, vmem_limit_bytes=58 * 2**20
        ),
        cost_estimate=pl.CostEstimate(
            flops=5_400_000_000, bytes_accessed=6_000_000, transcendentals=0
        ),
    )(hidden, down_weight, whitening)


def solution(mesh):
    placed = (P("mp", "dp", "tp"), P("mp", "tp", "dp"), P("mp", "dp", "tp"))
    return jax.shard_map(
        body, mesh=mesh, in_specs=placed, out_specs=P(("mp", "dp"), "tp"), check_vma=False
    )
```

time: 130 us -> 108 us (0.83)
  Pallas kernels: 127 us -> 105 us
    pallas_call x1, Pallas kernels: 127 us -> 105 us  [body(): pl.pallas_call(kernel, out_shape=jax.ShapeDtypeStruct((cols, cols), F32),...]
where the time goes in v2:
time: 108 us
  Pallas kernels  105 us (97%)
  local copies, waits for them, and re-layouts  2.26 us (2%)
    pallas_call x1, Pallas kernels, body(): pl.pallas_call(kernel, out_shape=jax.ShapeDtypeStruct((cols, cols), F32),...  105 us
    unnamed x1, local copies, waits for them, and re-layouts  2.26 us

profile of v2, /device:TPU:1, one launch (start us, length us, event | category | flops | bytes accessed | tf_op | source)
XLA Modules:
  0.0 107.6 jit_solution(6474896510278786123)
XLA Ops:
  0.0 105.3 %shard_map.37 = f32[512,512]{1,0:T(8,128)} custom-call(bf16[1,128,1792]{2,1,0:T(8,128)(2,1)} %hid.1, bf16[1,1792,1024]{2,1,0:T(8,128)(2,1)} %wgt.1, bf16[1,1024,512]{2,1,0:T(8,128)(2,1)} %fac.1), custom_call_target="tpu_custom_call" | custom-call | flops 5400000000 | bytes 6000000 | tf_op jit(solution)/shard_map/pallas_call | solution.py:386
  105.3 2.3 %copy.5 = f32[512,512]{1,0:T(8,128)} copy(f32[512,512]{1,0:T(8,128)} %shard_map.37) | data formatting | bytes 2097152

commit v3 on v2

--- a/solution.py
+++ b/solution.py
@@ -315,6 +315,14 @@
         value = value + land[2, d, cross].astype(F32)
     white[...] = value.astype(BF16)
 
+    def qwen_to(offsets):
+        for o, other in offsets:
+            send(
+                white, qwen.at[dp, mp], mp_sem, (other, o),
+                at(mp=1 - mp if other else mp, dp=rem(dp + o, 8)),
+            )
+
+    qwen_to(((1, 0), (7, 0), (2, 0), (6, 0), (3, 0), (5, 0), (4, 0)))
     @pl.when(jnp.logical_not(alone))
     def _():
         arrived(llama.at[z, core], row_sem, (0,))
@@ -328,13 +336,7 @@
 
     spreading = gather(spread, spread_sem, ())
     next(spreading)
-    for o in (4, 5, 3, 6, 2, 7, 1, 0):
-        for other in (1, 0):
-            if o or other:
-                send(
-                    white, qwen.at[dp, mp], mp_sem, (other, o),
-                    at(mp=1 - mp if other else mp, dp=rem(dp + o, 8)),
-                )
+    qwen_to(((0, 1), (1, 1), (7, 1), (2, 1), (6, 1), (3, 1), (5, 1), (4, 1)))
     qwen[dp, mp] = white[...]
 
     to_sibling((0,))
@@ -348,16 +350,24 @@
             if o or other:
                 source = qwen.at[rem(dp - o + 8, 8), 1 - mp if other else mp]
                 arrived(source, mp_sem, (other, o))
+    def half_of(part):
+        return llama[:, part].reshape(4 * tokens, cols), qwen[:, part].reshape(4 * tokens, cols)
+
+    def multiply(left, right, n):
+        return lax.dot_general(
+            left, right[:, n * TILE:(n + 1) * TILE], (((0,), (0,)), ((), ())), preferred_element_type=F32
+        )
+
+    left, right = half_of(core)
+    for n in range(cols // TILE):
+        out[:, pl.ds(n * TILE, TILE)] = multiply(left, right, n)
     for n in (0, -2, 2, -1, 1, -3, 3, -4):
         theirs = llama.at[rem(z - sign * n + 8, 8), 1 - core]
         arrived(theirs, last_sem, (n + 4,))
-    left = llama[...].reshape(8 * tokens, cols)
+    left, right = half_of(1 - core)
     for n in range(cols // TILE):
         here = pl.ds(n * TILE, TILE)
-        out[:, here] = lax.dot_general(
-            left, qwen[:, :, :, here].reshape(8 * tokens, TILE), (((0,), (0,)), ((), ())),
-            preferred_element_type=F32,
-        ) * (1.0 / math.sqrt(8 * tokens))
+        out[:, here] = (out[:, here] + multiply(left, right, n)) * (1.0 / math.sqrt(8 * tokens))
 
     for c in started:
         c.wait_send()

time: 108 us -> 105 us (0.972)
  Pallas kernels: 105 us -> 102 us
    pallas_call x1, Pallas kernels: 105 us -> 102 us  [body(): pl.pallas_call(kernel, out_shape=jax.ShapeDtypeStruct((cols, cols), F32),...]
where the time goes in v3:
time: 105 us
  Pallas kernels  102 us (97%)
  local copies, waits for them, and re-layouts  2.26 us (2%)
    pallas_call x1, Pallas kernels, body(): pl.pallas_call(kernel, out_shape=jax.ShapeDtypeStruct((cols, cols), F32),...  102 us
    unnamed x1, local copies, waits for them, and re-layouts  2.26 us

profile of v3, /device:TPU:1, one launch (start us, length us, event | category | flops | bytes accessed | tf_op | source)
XLA Modules:
  0.0 104.7 jit_solution(8685763388699419565)
XLA Ops:
  0.0 102.4 %shard_map.37 = f32[512,512]{1,0:T(8,128)} custom-call(bf16[1,128,1792]{2,1,0:T(8,128)(2,1)} %hid.1, bf16[1,1792,1024]{2,1,0:T(8,128)(2,1)} %wgt.1, bf16[1,1024,512]{2,1,0:T(8,128)(2,1)} %fac.1), custom_call_target="tpu_custom_call" | custom-call | flops 5400000000 | bytes 6000000 | tf_op jit(solution)/shard_map/pallas_call | solution.py:396
  102.4 2.3 %copy.5 = f32[512,512]{1,0:T(8,128)} copy(f32[512,512]{1,0:T(8,128)} %shard_map.37) | data formatting | bytes 2097152

commit v4 on v3

--- a/solution.py
+++ b/solution.py
@@ -322,7 +322,7 @@
                 at(mp=1 - mp if other else mp, dp=rem(dp + o, 8)),
             )
 
-    qwen_to(((1, 0), (7, 0), (2, 0), (6, 0), (3, 0), (5, 0), (4, 0)))
+    qwen_to(((1, 0), (7, 0), (2, 0), (6, 0), (3, 0), (5, 0), (4, 0), (0, 1), (1, 1), (7, 1)))
     @pl.when(jnp.logical_not(alone))
     def _():
         arrived(llama.at[z, core], row_sem, (0,))
@@ -336,7 +336,7 @@
 
     spreading = gather(spread, spread_sem, ())
     next(spreading)
-    qwen_to(((0, 1), (1, 1), (7, 1), (2, 1), (6, 1), (3, 1), (5, 1), (4, 1)))
+    qwen_to(((2, 1), (6, 1), (3, 1), (5, 1), (4, 1)))
     qwen[dp, mp] = white[...]
 
     to_sibling((0,))

time: 105 us -> 104 us (level)
  no operation moved by 1% of the time
where the time goes in v4:
time: 104 us
  Pallas kernels  102 us (98%)
  local copies, waits for them, and re-layouts  2.26 us (2%)
    pallas_call x1, Pallas kernels, body(): pl.pallas_call(kernel, out_shape=jax.ShapeDtypeStruct((cols, cols), F32),...  102 us
    unnamed x1, local copies, waits for them, and re-layouts  2.26 us

profile of v4, /device:TPU:1, one launch (start us, length us, event | category | flops | bytes accessed | tf_op | source)
XLA Modules:
  0.0 103.9 jit_solution(3154463331827108315)
XLA Ops:
  0.0 101.6 %shard_map.37 = f32[512,512]{1,0:T(8,128)} custom-call(bf16[1,128,1792]{2,1,0:T(8,128)(2,1)} %hid.1, bf16[1,1792,1024]{2,1,0:T(8,128)(2,1)} %wgt.1, bf16[1,1024,512]{2,1,0:T(8,128)(2,1)} %fac.1), custom_call_target="tpu_custom_call" | custom-call | flops 5400000000 | bytes 6000000 | tf_op jit(solution)/shard_map/pallas_call | solution.py:396
  101.6 2.3 %copy.5 = f32[512,512]{1,0:T(8,128)} copy(f32[512,512]{1,0:T(8,128)} %shard_map.37) | data formatting | bytes 2097152

commit v5 on v4

--- a/solution.py
+++ b/solution.py
@@ -87,6 +87,14 @@
     loads[0].wait()
     sums[dp] = jnp.sum(acts[pl.ds(row0, tokens), :].astype(F32), axis=0, keepdims=True)
 
+    loads[1].wait()
+    for dst, first in ((give, (1 - core) * side), (own, core * side)):
+        for n in range(side // TILE):
+            columns = pl.ds(pl.multiple_of(first + n * TILE, TILE), TILE)
+            dst[0, pl.ds(0, tokens), pl.ds(n * TILE, TILE)] = jnp.dot(
+                acts[pl.ds(row0, tokens), :], weights[:, columns], preferred_element_type=F32
+            )
+
     extra = jnp.where(mp == 0, jnp.where(alone, 1, 2), 0)
     pl.semaphore_wait(barrier, len(greet) + extra)
 
@@ -124,7 +132,6 @@
     for index in (10, 0, 5, 11, 1, 6):
         hop(index)
 
-    loads[1].wait()
     for o in range(1, 8):
         arrived(sums.at[rem(dp - o, 8)], sum_sem, (o,))
     mean = jnp.sum(sums[...], axis=0) * (1.0 / 1024)
@@ -170,6 +177,9 @@
             landed(index)
 
         def partial(dst, first, offset):
+            if g == 0:
+                dst[g, span, :] = dst[g, span, :] - offset
+                return
             for n in range(side // TILE):
                 columns = pl.ds(pl.multiple_of(first + n * TILE, TILE), TILE)
                 dst[g, span, pl.ds(n * TILE, TILE)] = (

time: 104 us -> 105 us (level)
  no operation moved by 1% of the time
where the time goes in v5:
time: 105 us; the launch traced here: 104 us
  Pallas kernels  102 us (97%)
  local copies, waits for them, and re-layouts  2.26 us (2%)
    pallas_call x1, Pallas kernels, body(): pl.pallas_call(kernel, out_shape=jax.ShapeDtypeStruct((cols, cols), F32),...  102 us
    unnamed x1, local copies, waits for them, and re-layouts  2.26 us

profile of v5, /device:TPU:1, one launch (start us, length us, event | category | flops | bytes accessed | tf_op | source)
XLA Modules:
  0.0 104.1 jit_solution(1197514041906478348)
XLA Ops:
  0.0 101.9 %shard_map.37 = f32[512,512]{1,0:T(8,128)} custom-call(bf16[1,128,1792]{2,1,0:T(8,128)(2,1)} %hid.1, bf16[1,1792,1024]{2,1,0:T(8,128)(2,1)} %wgt.1, bf16[1,1024,512]{2,1,0:T(8,128)(2,1)} %fac.1), custom_call_target="tpu_custom_call" | custom-call | flops 5400000000 | bytes 6000000 | tf_op jit(solution)/shard_map/pallas_call | solution.py:406
  101.9 2.3 %copy.5 = f32[512,512]{1,0:T(8,128)} copy(f32[512,512]{1,0:T(8,128)} %shard_map.37) | data formatting | bytes 2097152
